TPU v7x, 256 devices: a whole 4x4x8 slice. The times are simulated.
256 devices in a mesh: section: 32 (over z_lo, y, core), expert: 8 (over x, z_hi).
Axes of the slice: x: 4, y: 4, z: 8 (z_hi: 2, z_lo: 4; z = z_hi * 4 + z_lo), core: 2. Of those that a mesh axis runs over, the one named last changes fastest.
Arguments:
- forward_in: bfloat16 [32, 512, 7168], P('section', 'expert'), may hold values from -6 to 6
- entering: bfloat16 [1, 512, 7168], P(None, 'expert'), may hold values from -6 to 6
- cotangent_in: bfloat16 [32, 512, 7168], P('section', 'expert'), may hold values from -6 to 6
- cot_entering: bfloat16 [1, 512, 7168], P(None, 'expert'), may hold values from -6 to 6
- stash: bfloat16 [2, 32, 512, 7168], P(None, 'section', 'expert'), may hold values from -6 to 6
- norm_gain: float32 [32, 7168], P('section'), may hold values from 0.5 to 1.5
- w_gate: bfloat16 [32, 1, 7168, 1024], P('section', None, None, 'expert'), may hold values from -0.0625 to 0.0625
- w_up: bfloat16 [32, 1, 7168, 1024], P('section', None, None, 'expert'), may hold values from -0.0625 to 0.0625
- w_down: bfloat16 [32, 1, 1024, 7168], P('section', None, 'expert'), may hold values from -0.1875 to 0.1875
- ids_fwd: int32 [2, 32, 512, 8], P(None, 'section'), may hold values from 0 to 255, as said below
- route_fwd: float32 [2, 32, 512, 8], P(None, 'section'), may hold values from 0.25 to 1.5
- ids_bwd: int32 [2, 32, 512, 8], P(None, 'section'), may hold values from 0 to 255, as said below
- route_bwd: float32 [2, 32, 512, 8], P(None, 'section'), may hold values from 0.25 to 1.5
Outputs:
- forward_out: bfloat16 [32, 512, 7168], P('section', 'expert')
- cotangent_out: bfloat16 [32, 512, 7168], P('section', 'expert')
Inputs may be any that keep to these rules, and one draw needn't show every extreme that they name: `ids_fwd`: each row names 8 different experts. Among the 64 rows of one index of expert (aligned blocks of the token dimension), from 1 to 16 rows name any one expert below 1; for each such expert some step and layer have exactly 16 such rows on every index of expert. `ids_bwd`: as for ids_fwd.
All inputs are finite; a program needn't handle non-finite values.
Results may differ from a plain program's by a relative error of at most 0.006.
Values may be sent and summed in bfloat16 or wider, within the bound.
No kernel may reach another device: no remote copies, remote signals or barrier semaphores. Data moves between devices by JAX's collectives and lax.ppermute only.
A program may use at most 128 MiB of HBM per device.

v0:
```python
import jax
import jax.numpy as jnp
from jax import lax
from jax.sharding import PartitionSpec as P

CAP = 16
EPSILON = 1e-06


def from_behind(block, axis, distance):
    devices = range(lax.axis_size(axis))
    route = [(i - distance, i) for i in devices if i - distance in devices]
    return lax.ppermute(block, axis, route)


def routing_plan(ids, weights, flight, groups, capacity, own_index):
    experts = jnp.arange(flight, dtype=jnp.int32)
    matches = (ids[:, :, None] == experts[None, None, :]).astype(jnp.float32)
    mixing = jnp.sum(weights[:, :, None] * matches, axis=1)
    member = (jnp.sum(matches, axis=1) > 0).astype(jnp.int32).reshape(groups, -1, flight)
    slot_of = jnp.cumsum(member, axis=1) - 1
    slot_ids = jnp.arange(capacity, dtype=jnp.int32)
    one_hot = ((member[..., None] == 1) & (slot_of[..., None] == slot_ids)).astype(jnp.float32)
    pack_all = jnp.transpose(one_hot, (2, 0, 3, 1))
    mix_blocks = jnp.transpose(mixing.reshape(groups, -1, flight), (2, 0, 1))
    slot_weight = jnp.sum(pack_all * mix_blocks[:, :, None, :], axis=3)
    own_pack = lax.dynamic_index_in_dim(pack_all, own_index, 1, keepdims=False)
    return (own_pack, slot_weight.reshape(flight, groups * capacity))


def pack_rows(own_pack, source):
    return jnp.einsum(
        "ect,td->ecd", own_pack.astype(jnp.bfloat16), source, preferred_element_type=jnp.float32
    ).astype(jnp.bfloat16)


def unpack_rows(own_pack, summed):
    return jnp.einsum(
        "ect,ecd->td",
        own_pack,
        summed,
        precision=lax.Precision.HIGHEST,
        preferred_element_type=jnp.float32,
    )


def norm_pieces(source, norm_scale):
    row_floats = source.astype(jnp.float32)
    inverse_root_square = lax.rsqrt(
        jnp.mean(row_floats * row_floats, axis=-1, keepdims=True) + EPSILON
    )
    centered_input = row_floats * inverse_root_square
    return ((centered_input * norm_scale).astype(jnp.bfloat16), centered_input, inverse_root_square)


def expert_forward(packed, gate_dev, up_dev, down_dev, slot_weight):
    gate_pre = jnp.einsum("erd,edf->erf", packed, gate_dev, preferred_element_type=jnp.float32)
    up_pre = jnp.einsum("erd,edf->erf", packed, up_dev, preferred_element_type=jnp.float32)
    hidden = (gate_pre * jax.nn.sigmoid(gate_pre) * up_pre).astype(jnp.bfloat16)
    outputs = jnp.einsum("erf,efd->erd", hidden, down_dev, preferred_element_type=jnp.float32)
    return slot_weight[:, :, None] * outputs


def expert_backward(packed, cot_packed, gate_dev, up_dev, down_dev, slot_weight):
    gate_pre = jnp.einsum("erd,edf->erf", packed, gate_dev, preferred_element_type=jnp.float32)
    up_pre = jnp.einsum("erd,edf->erf", packed, up_dev, preferred_element_type=jnp.float32)
    sigma = jax.nn.sigmoid(gate_pre)
    activated = gate_pre * sigma
    expert_cot = (slot_weight[:, :, None] * cot_packed.astype(jnp.float32)).astype(jnp.bfloat16)
    hidden_cot = jnp.einsum(
        "erd,efd->erf", expert_cot, down_dev, preferred_element_type=jnp.float32
    )
    gate_cot = (hidden_cot * up_pre * sigma * (1.0 + gate_pre * (1.0 - sigma))).astype(jnp.bfloat16)
    up_cot = (hidden_cot * activated).astype(jnp.bfloat16)
    partial_cot = jnp.einsum("erf,edf->erd", gate_cot, gate_dev, preferred_element_type=jnp.float32)
    return partial_cot + jnp.einsum(
        "erf,edf->erd", up_cot, up_dev, preferred_element_type=jnp.float32
    )


def on_device(
    forward_in,
    entering,
    cotangent_in,
    cot_entering,
    stash,
    norm_gain,
    w_gate,
    w_up,
    w_down,
    ids_fwd,
    route_fwd,
    ids_bwd,
    route_bwd,
):
    section_index = lax.axis_index("section")
    last_section = lax.axis_size("section") - 1
    groups = lax.axis_size("expert")
    own_index = lax.axis_index("expert")
    scale_row_vector = norm_gain[0]
    gate_dev = w_gate[0]
    up_dev = w_up[0]
    down_dev = w_down[0]
    flight = gate_dev.shape[0]
    step_count = stash.shape[0]
    forward_token_rows = forward_in[0]
    cot_rows = cotangent_in[0]
    next_fwd = forward_token_rows
    next_cot = cot_rows
    for tick_index in range(step_count):
        own_fwd, weight_fwd = routing_plan(
            ids_fwd[tick_index, 0], route_fwd[tick_index, 0], flight, groups, CAP, own_index
        )
        own_bwd, weight_bwd = routing_plan(
            ids_bwd[tick_index, 0], route_bwd[tick_index, 0], flight, groups, CAP, own_index
        )
        normalized_forward, centered_forward, root_square_forward = norm_pieces(
            forward_token_rows, scale_row_vector
        )
        normalized_backward, centered_backward, root_square_backward = norm_pieces(
            stash[tick_index, 0], scale_row_vector
        )
        packed_fwd = pack_rows(own_fwd, normalized_forward)
        packed_bwd = pack_rows(own_bwd, normalized_backward)
        packed_cot = pack_rows(own_bwd, cot_rows)
        whole_fwd, whole_bwd, whole_cot = (
            lax.all_gather(packed_fwd, "expert", axis=1, tiled=True),
            lax.all_gather(packed_bwd, "expert", axis=1, tiled=True),
            lax.all_gather(packed_cot, "expert", axis=1, tiled=True),
        )
        partial_fwd = expert_forward(whole_fwd, gate_dev, up_dev, down_dev, weight_fwd)
        partial_bwd = expert_backward(whole_bwd, whole_cot, gate_dev, up_dev, down_dev, weight_bwd)
        sum_fwd, sum_bwd = (
            lax.psum_scatter(partial_fwd, "expert", scatter_dimension=1, tiled=True),
            lax.psum_scatter(partial_bwd, "expert", scatter_dimension=1, tiled=True),
        )
        next_fwd = (forward_token_rows.astype(jnp.float32) + unpack_rows(own_fwd, sum_fwd)).astype(
            jnp.bfloat16
        )
        scaled_rows = unpack_rows(own_bwd, sum_bwd) * scale_row_vector
        next_cot = cot_rows.astype(jnp.float32) + root_square_backward * (
            scaled_rows
            - centered_backward * jnp.mean(scaled_rows * centered_backward, axis=-1, keepdims=True)
        )
        next_cot = next_cot.astype(jnp.bfloat16)
        if tick_index + 1 < step_count:
            moved_fwd = from_behind(next_fwd, "section", 1)
            moved_cot = from_behind(next_cot, "section", -1)
            forward_token_rows = jnp.where(section_index == 0, entering[tick_index], moved_fwd)
            cot_rows = jnp.where(section_index == last_section, cot_entering[tick_index], moved_cot)
    return (next_fwd[None], next_cot[None])


def solution(mesh):
    placed = (
        P("section", "expert", None),
        P(None, "expert", None),
        P("section", "expert", None),
        P(None, "expert", None),
        P(None, "section", "expert", None),
        P("section", None),
        P("section", None, None, "expert"),
        P("section", None, None, "expert"),
        P("section", None, "expert", None),
        P(None, "section", None, None),
        P(None, "section", None, None),
        P(None, "section", None, None),
        P(None, "section", None, None),
    )
    return jax.shard_map(
        on_device,
        mesh=mesh,
        in_specs=placed,
        out_specs=(P("section", "expert", None), P("section", "expert", None)),
        check_vma=False,
    )
```

profile of v0, /device:TPU:8, one launch (start us, length us, event | category | flops | bytes accessed | tf_op | source)
XLA Modules:
  0.0 941.1 jit_solution(7283005679157287276)
XLA Ops:
  7.2 0.9 slice_compare_fusion.1
  8.1 0.8 select_reduce_fusion.4
  9.2 1.5 fusion.31
  10.8 2.3 convolution_convert_fusion.2
  13.1 0.9 convolution_convert_fusion.3
  14.3 0.2 reduce_window_sum.22
  14.5 1.5 fusion.28
  16.1 2.3 convolution_convert_fusion.5
  18.7 70.1 %all-gather.19.cloned.1.call-done = bf16[128,7168]{1,0:T(8,128)(2,1)} async-done(((bf16[16,7168]{1,0:T(8,128)(2,1)}), bf16[128,7168]{1,0:T(8,128)(2,1)}) %all-gather.19.cloned.1.call-update) | async-done | bytes 1835024 | tf_op jit(solution)/shard_map/all_gather | solution.py:128
  88.8 2.7 fusion.68
  91.5 68.7 %all-gather.17.cloned.1.call-done = bf16[128,7168]{1,0:T(8,128)(2,1)} async-done(((bf16[16,7168]{1,0:T(8,128)(2,1)}), bf16[128,7168]{1,0:T(8,128)(2,1)}) %all-gather.17.cloned.1.call-update) | async-done | bytes 1835024 | tf_op jit(solution)/shard_map/all_gather | solution.py:129
  160.2 2.7 fusion.41
  163.0 5.1 fusion.66
  168.1 4.5 fusion.1
  172.9 58.7 %all-gather.13.cloned.1.call-done = bf16[128,7168]{1,0:T(8,128)(2,1)} async-done(((bf16[16,7168]{1,0:T(8,128)(2,1)}), bf16[128,7168]{1,0:T(8,128)(2,1)}) %all-gather.13.cloned.1.call-update) | async-done | bytes 1835024 | tf_op jit(solution)/shard_map/all_gather | solution.py:127
  231.6 2.7 fusion.72
  234.3 5.1 fusion.3
  239.5 0.2 reduce_window_sum.32
  239.8 112.7 %reduce-scatter.9.cloned.1.call-done = f32[1,16,7168]{2,1,0:T(8,128)} async-done(((f32[1,128,7168]{2,1,0:T(8,128)}), f32[1,16,7168]{2,1,0:T(8,128)}) %reduce-scatter.9.cloned.1.call-update) | async-done | bytes 458768 | tf_op jit(solution)/shard_map/reduce_scatter | solution.py:135
  352.5 4.4 fusion.34
  356.9 1.1 convolution_convert_fusion
  358.0 3.5 fusion.27
  361.6 1.9 collective-permute-start.1
  363.5 11.2 %collective-permute-done.1 = bf16[64,7168]{1,0:T(8,128)(2,1)} collective-permute-done((bf16[64,7168]{1,0:T(8,128)(2,1)}, bf16[64,7168]{1,0:T(8,128)(2,1)}, u32[]{:S(2)}, u32[]{:S(2)}) %collective-permute-start.1) | collective-permute-done | bytes 917536 | tf_op jit(solution)/shard_map/ppermute | solution.py:13
  374.7 2.2 convolution_convert_fusion.1
  377.0 95.4 %reduce-scatter.5.cloned.1.call-done = f32[1,16,7168]{2,1,0:T(8,128)} async-done(((f32[1,128,7168]{2,1,0:T(8,128)}), f32[1,16,7168]{2,1,0:T(8,128)}) %reduce-scatter.5.cloned.1.call-update) | async-done | bytes 458768 | tf_op jit(solution)/shard_map/reduce_scatter | solution.py:134
  472.3 3.2 fusion.4
  475.5 1.9 collective-permute-start
  477.5 0.2 reduce_window_sum.23
  477.8 12.8 %collective-permute-done = bf16[64,7168]{1,0:T(8,128)(2,1)} collective-permute-done((bf16[64,7168]{1,0:T(8,128)(2,1)}, bf16[64,7168]{1,0:T(8,128)(2,1)}, u32[]{:S(2)}, u32[]{:S(2)}) %collective-permute-start) | collective-permute-done | bytes 917536 | tf_op jit(solution)/shard_map/ppermute | solution.py:13
  490.5 1.9 fusion.37
  492.5 0.9 copy-done.5
  493.4 1.1 convolution_convert_fusion.4
  494.5 0.2 reduce-scatter.11.cloned.1.call-start
  495.0 48.2 %all-gather.23.cloned.1.call-done = bf16[128,7168]{1,0:T(8,128)(2,1)} async-done(((bf16[16,7168]{1,0:T(8,128)(2,1)}), bf16[128,7168]{1,0:T(8,128)(2,1)}) %all-gather.23.cloned.1.call-update) | async-done | bytes 1835024 | tf_op jit(solution)/shard_map/all_gather | solution.py:128
  543.2 2.7 fusion.64
  545.9 68.1 %all-gather.21.cloned.1.call-done = bf16[128,7168]{1,0:T(8,128)(2,1)} async-done(((bf16[16,7168]{1,0:T(8,128)(2,1)}), bf16[128,7168]{1,0:T(8,128)(2,1)}) %all-gather.21.cloned.1.call-update) | async-done | bytes 1835024 | tf_op jit(solution)/shard_map/all_gather | solution.py:129
  614.0 2.7 fusion.44
  616.8 5.1 fusion.62
  621.9 4.5 fusion
  626.7 58.7 %all-gather.15.cloned.1.call-done = bf16[128,7168]{1,0:T(8,128)(2,1)} async-done(((bf16[16,7168]{1,0:T(8,128)(2,1)}), bf16[128,7168]{1,0:T(8,128)(2,1)}) %all-gather.15.cloned.1.call-update) | async-done | bytes 1835024 | tf_op jit(solution)/shard_map/all_gather | solution.py:127
  685.4 2.7 fusion.70
  688.1 5.1 fusion.2
  693.2 113.2 %reduce-scatter.11.cloned.1.call-done = f32[1,16,7168]{2,1,0:T(8,128)} async-done(((f32[1,128,7168]{2,1,0:T(8,128)}), f32[1,16,7168]{2,1,0:T(8,128)}) %reduce-scatter.11.cloned.1.call-update) | async-done | bytes 458768 | tf_op jit(solution)/shard_map/reduce_scatter | solution.py:135
  806.4 3.8 fusion.18
  810.2 117.5 %reduce-scatter.7.cloned.1.call-done = f32[1,16,7168]{2,1,0:T(8,128)} async-done(((f32[1,128,7168]{2,1,0:T(8,128)}), f32[1,16,7168]{2,1,0:T(8,128)}) %reduce-scatter.7.cloned.1.call-update) | async-done | bytes 458768 | tf_op jit(solution)/shard_map/reduce_scatter | solution.py:134
  927.7 3.3 fusion.6
  931.0 3.3 fusion.123
  (75 shorter events, 2.3 us)
Async XLA Ops:
  7.2 155.8 %copy-start = (bf16[1,1,7168,128]{3,2,1,0:T(8,128)(2,1)S(1)}, bf16[1,1,7168,128]{3,2,1,0:T(8,128)(2,1)}, u32[]{:S(2)}) copy-start(bf16[1,1,7168,128]{3,2,1,0:T(8,128)(2,1)} %param.20) | copy-start | bytes 5505028
  7.2 6.0 copy-start.4
  7.2 81.6 %all-gather.19.cloned.1.call-start = ((), (), s32[]{:S(2)}) async-start(), calls=%async_computation.11 | async-start | bytes 2064384 | tf_op jit(solution)/shard_map/all_gather | solution.py:128
  10.7 3.5 copy-start.6
  10.7 3.5 copy-start.7
  10.8 5.3 copy-start.8
  13.1 147.1 %all-gather.17.cloned.1.call-start = ((), (), s32[]{:S(2)}) async-start(), calls=%async_computation.10 | async-start | bytes 2064384 | tf_op jit(solution)/shard_map/all_gather | solution.py:129
  14.1 217.5 %all-gather.13.cloned.1.call-start = ((), (), s32[]{:S(2)}) async-start(), calls=%async_computation.8 | async-start | bytes 2064384 | tf_op jit(solution)/shard_map/all_gather | solution.py:127
  18.4 334.1 %reduce-scatter.9.cloned.1.call-start = ((), (), s32[]{:S(2)}) async-start(), calls=%async_computation.6 | async-start | bytes 4128768 | tf_op jit(solution)/shard_map/reduce_scatter | solution.py:135
  172.6 299.7 %reduce-scatter.5.cloned.1.call-start = ((), (), s32[]{:S(2)}) async-start(), calls=%async_computation.4 | async-start | bytes 4128768 | tf_op jit(solution)/shard_map/reduce_scatter | solution.py:134
  239.4 303.8 %all-gather.23.cloned.1.call-start = ((), (), s32[]{:S(2)}) async-start(), calls=%async_computation.13 | async-start | bytes 2064384 | tf_op jit(solution)/shard_map/all_gather | solution.py:128
  352.5 4.4 copy-start.1
  358.0 256.0 %all-gather.21.cloned.1.call-start = ((), (), s32[]{:S(2)}) async-start(), calls=%async_computation.12 | async-start | bytes 2064384 | tf_op jit(solution)/shard_map/all_gather | solution.py:129
  358.0 16.7 %copy-start.3 = (bf16[1,64,7168]{2,1,0:T(8,128)(2,1)S(1)}, bf16[1,64,7168]{2,1,0:T(8,128)(2,1)}, u32[]{:S(2)}) copy-start(bf16[1,64,7168]{2,1,0:T(8,128)(2,1)} %param.16) | copy-start | bytes 2752516
  361.6 13.1 %collective-permute-start.1 = (bf16[64,7168]{1,0:T(8,128)(2,1)}, bf16[64,7168]{1,0:T(8,128)(2,1)}, u32[]{:S(2)}, u32[]{:S(2)}) collective-permute-start(bf16[64,7168]{1,0:T(8,128)(2,1)} %fusion.27), channel_id=1, source_target_pairs={{8,0},{16,8},{24,16},{32,24},{40,32},{48,40},{56,48},{64,56},{72,6... | collective-permute-start | bytes 2752520 | tf_op jit(solution)/shard_map/ppermute | solution.py:13
  376.9 308.5 %all-gather.15.cloned.1.call-start = ((), (), s32[]{:S(2)}) async-start(), calls=%async_computation.9 | async-start | bytes 2064384 | tf_op jit(solution)/shard_map/all_gather | solution.py:127
  475.5 15.0 %collective-permute-start = (bf16[64,7168]{1,0:T(8,128)(2,1)}, bf16[64,7168]{1,0:T(8,128)(2,1)}, u32[]{:S(2)}, u32[]{:S(2)}) collective-permute-start(bf16[64,7168]{1,0:T(8,128)(2,1)} %fusion.4), channel_id=1, source_target_pairs={{0,8},{8,16},{16,24},{24,32},{32,40},{40,48},{48,56},{56,64},{64,7... | collective-permute-start | bytes 2752520 | tf_op jit(solution)/shard_map/ppermute | solution.py:13
  492.4 0.9 copy-start.5
  494.5 311.9 %reduce-scatter.11.cloned.1.call-start = ((), (), s32[]{:S(2)}) async-start(), calls=%async_computation.7 | async-start | bytes 4128768 | tf_op jit(solution)/shard_map/reduce_scatter | solution.py:135
  626.4 301.3 %reduce-scatter.7.cloned.1.call-start = ((), (), s32[]{:S(2)}) async-start(), calls=%async_computation.5 | async-start | bytes 4128768 | tf_op jit(solution)/shard_map/reduce_scatter | solution.py:134
  927.7 3.3 copy-start.2
Sparse Core Ops, SparseCore 0:
  13.2 75.5 all-gather.18
  92.0 68.1 all-gather.16
  163.4 68.1 all-gather.12
  235.7 116.6 reduce-scatter.8
  357.2 115.1 reduce-scatter.4
  474.8 68.3 all-gather.22
  545.8 68.1 all-gather.20
  617.2 68.1 all-gather.14
  689.7 116.6 reduce-scatter.10
  811.1 116.5 reduce-scatter.6
where the time goes:
time: 942 us; the launch traced here: 941 us
  waiting for transfers between devices  836 us (89%)
  matrix products  70.1 us (7%)
  other arithmetic  14.7 us (2%)
  between operations  14.5 us (2%)
    reduce_scatter x2, waiting for transfers between devices, on_device(): lax.psum_scatter(partial_bwd, 'expert', scatter_dimension=1, tiled=True)  226 us
    reduce_scatter x2, waiting for transfers between devices, on_device(): lax.psum_scatter(partial_fwd, 'expert', scatter_dimension=1, tiled=True)  213 us
    all_gather x2, waiting for transfers between devices, on_device(): lax.all_gather(packed_cot, 'expert', axis=1, tiled=True)  137 us
    all_gather x2, waiting for transfers between devices, on_device(): lax.all_gather(packed_bwd, 'expert', axis=1, tiled=True)  118 us
    all_gather x2, waiting for transfers between devices, on_device(): lax.all_gather(packed_fwd, 'expert', axis=1, tiled=True)  117 us
    ppermute x2, waiting for transfers between devices, from_behind(): return lax.ppermute(block, axis, route)  24 us
  transfers between devices with their start and end apart: 12, of which 12 were waited for; matrix products, arithmetic and copies ran while one was open for 8% of the time, Pallas kernels for 0%

commit v1 on v0

--- a/solution.py
+++ b/solution.py
@@ -124,7 +124,10 @@
         packed_bwd = pack_rows(own_bwd, normalized_backward)
         packed_cot = pack_rows(own_bwd, cot_rows)
         whole_fwd, whole_bwd, whole_cot = (
-            lax.all_gather(packed_fwd, "expert", axis=1, tiled=True),
+            jnp.concatenate(
+                lax.all_to_all(jnp.stack([packed_fwd] * lax.axis_size("expert")), "expert", 0, 0),
+                axis=1,
+            ),
             lax.all_gather(packed_bwd, "expert", axis=1, tiled=True),
             lax.all_gather(packed_cot, "expert", axis=1, tiled=True),
         )

time: 942 us -> 860 us (0.913)
  waiting for transfers between devices: 836 us -> 745 us
    all_gather x2 -> x0, waiting for transfers between devices: 117 us -> none  [on_device(): lax.all_gather(packed_fwd, 'expert', axis=1, tiled=True)]
    all_to_all x0 -> x2, waiting for transfers between devices: none -> 104 us  [on_device(): lax.all_to_all(jnp.stack([packed_fwd] * lax.axis_size('expert')), 'expert...]
    all_gather x2, waiting for transfers between devices: 118 us -> 74.3 us  [on_device(): lax.all_gather(packed_bwd, 'expert', axis=1, tiled=True)]
    reduce_scatter x2, waiting for transfers between devices: 226 us -> 186 us  [on_device(): lax.psum_scatter(partial_bwd, 'expert', scatter_dimension=1, tiled=True)]
    reduce_scatter x2, waiting for transfers between devices: 213 us -> 226 us  [on_device(): lax.psum_scatter(partial_fwd, 'expert', scatter_dimension=1, tiled=True)]
  transfers between devices with their start and end apart: 12 -> 12, of which waited for: 12 -> 11; matrix products, arithmetic and copies ran while one was open for 8% -> 6% of each run, Pallas kernels for 0% -> 0%
where the time goes in v1:
time: 860 us
  waiting for transfers between devices  745 us (87%)
  matrix products  67.5 us (8%)
  between operations  14.5 us (2%)
  other arithmetic  14.4 us (2%)
  starting transfers between devices  13.1 us (2%)
    reduce_scatter x2, waiting for transfers between devices, on_device(): lax.psum_scatter(partial_fwd, 'expert', scatter_dimension=1, tiled=True)  226 us
    reduce_scatter x2, waiting for transfers between devices, on_device(): lax.psum_scatter(partial_bwd, 'expert', scatter_dimension=1, tiled=True)  186 us
    all_gather x2, waiting for transfers between devices, on_device(): lax.all_gather(packed_cot, 'expert', axis=1, tiled=True)  138 us
    all_to_all x2, waiting for transfers between devices, on_device(): lax.all_to_all(jnp.stack([packed_fwd] * lax.axis_size('expert')), 'expert...  104 us
    all_gather x2, waiting for transfers between devices, on_device(): lax.all_gather(packed_bwd, 'expert', axis=1, tiled=True)  74.3 us
    ppermute x2, waiting for transfers between devices, from_behind(): return lax.ppermute(block, axis, route)  17.6 us
  transfers between devices with their start and end apart: 12, of which 11 were waited for; matrix products, arithmetic and copies ran while one was open for 6% of the time, Pallas kernels for 0%

profile of v1, /device:TPU:8, one launch (start us, length us, event | category | flops | bytes accessed | tf_op | source)
XLA Modules:
  0.0 859.6 jit_solution(6427437001944587585)
XLA Ops:
  7.2 0.9 slice_compare_fusion.1
  8.1 0.8 select_reduce_fusion.4
  9.2 1.5 fusion.31
  10.7 2.3 convolution_convert_fusion.2
  13.1 0.9 convolution_convert_fusion.3
  14.4 74.3 %all-gather.11.cloned.1.call-done = bf16[128,7168]{1,0:T(8,128)(2,1)} async-done(((bf16[16,7168]{1,0:T(8,128)(2,1)}), bf16[128,7168]{1,0:T(8,128)(2,1)}) %all-gather.11.cloned.1.call-update) | async-done | bytes 1835024 | tf_op jit(solution)/shard_map/all_gather | solution.py:131
  88.7 2.7 fusion.68
  91.4 68.7 %all-gather.9.cloned.1.call-done = bf16[128,7168]{1,0:T(8,128)(2,1)} async-done(((bf16[16,7168]{1,0:T(8,128)(2,1)}), bf16[128,7168]{1,0:T(8,128)(2,1)}) %all-gather.9.cloned.1.call-update) | async-done | bytes 1835024 | tf_op jit(solution)/shard_map/all_gather | solution.py:132
  160.1 2.7 fusion.41
  162.9 5.1 fusion.66
  168.0 4.5 fusion.1
  172.8 0.4 copy-done.7
  173.6 1.5 fusion.28
  175.1 114.2 %reduce-scatter.9.cloned.1.call-done = f32[1,16,7168]{2,1,0:T(8,128)} async-done(((f32[1,128,7168]{2,1,0:T(8,128)}), f32[1,16,7168]{2,1,0:T(8,128)}) %reduce-scatter.9.cloned.1.call-update) | async-done | bytes 458768 | tf_op jit(solution)/shard_map/reduce_scatter | solution.py:138
  289.3 4.4 fusion.34
  293.7 1.1 convolution_convert_fusion
  294.8 3.2 fusion.27
  298.1 1.9 collective-permute-start.1
  300.1 0.4 convolution_convert_fusion.5
  300.4 1.4 stack.4
  301.9 4.5 all-to-all-start
  306.4 4.8 collective-permute-done.1
  311.2 2.2 convolution_convert_fusion.1
  313.7 61.6 %all-to-all-done = bf16[8,1,16,7168]{3,2,1,0:T(8,128)(2,1)} async-done(((bf16[8,1,16,7168]{3,2,1,0:T(8,128)(2,1)}), bf16[8,1,16,7168]{3,2,1,0:T(8,128)(2,1)}, u32[]{:S(2)}, u32[]{:S(2)}) %all-to-all-start) | async-done | bytes 1835040 | tf_op jit(solution)/shard_map/all_to_all | solution.py:128
  375.3 2.7 fusion.72
  378.0 5.1 fusion.3
  383.7 2.7 fusion.64
  386.3 69.1 %all-gather.13.cloned.1.call-done = bf16[128,7168]{1,0:T(8,128)(2,1)} async-done(((bf16[16,7168]{1,0:T(8,128)(2,1)}), bf16[128,7168]{1,0:T(8,128)(2,1)}) %all-gather.13.cloned.1.call-update) | async-done | bytes 1835024 | tf_op jit(solution)/shard_map/all_gather | solution.py:132
  455.4 2.7 fusion.44
  458.2 5.0 fusion.62
  463.2 4.5 fusion
  467.7 109.1 %reduce-scatter.5.cloned.1.call-done = f32[1,16,7168]{2,1,0:T(8,128)} async-done(((f32[1,128,7168]{2,1,0:T(8,128)}), f32[1,16,7168]{2,1,0:T(8,128)}) %reduce-scatter.5.cloned.1.call-update) | async-done | bytes 458768 | tf_op jit(solution)/shard_map/reduce_scatter | solution.py:137
  576.7 3.2 fusion.4
  580.0 1.9 collective-permute-start
  582.2 12.8 %collective-permute-done = bf16[64,7168]{1,0:T(8,128)(2,1)} collective-permute-done((bf16[64,7168]{1,0:T(8,128)(2,1)}, bf16[64,7168]{1,0:T(8,128)(2,1)}, u32[]{:S(2)}, u32[]{:S(2)}) %collective-permute-start) | collective-permute-done | bytes 917536 | tf_op jit(solution)/shard_map/ppermute | solution.py:13
  595.0 1.9 fusion.37
  596.9 0.9 copy-done.6
  597.8 0.4 convolution_convert_fusion.4
  598.2 1.5 stack.5
  599.7 4.3 all-to-all-start.1
  604.3 42.3 %all-to-all-done.1 = bf16[8,1,16,7168]{3,2,1,0:T(8,128)(2,1)} async-done(((bf16[8,1,16,7168]{3,2,1,0:T(8,128)(2,1)}), bf16[8,1,16,7168]{3,2,1,0:T(8,128)(2,1)}, u32[]{:S(2)}, u32[]{:S(2)}) %all-to-all-start.1) | async-done | bytes 1835040 | tf_op jit(solution)/shard_map/all_to_all | solution.py:128
  646.6 2.7 fusion.70
  649.2 5.1 fusion.2
  654.4 71.5 %reduce-scatter.11.cloned.1.call-done = f32[1,16,7168]{2,1,0:T(8,128)} async-done(((f32[1,128,7168]{2,1,0:T(8,128)}), f32[1,16,7168]{2,1,0:T(8,128)}) %reduce-scatter.11.cloned.1.call-update) | async-done | bytes 458768 | tf_op jit(solution)/shard_map/reduce_scatter | solution.py:138
  725.8 3.8 fusion.18
  729.7 116.5 %reduce-scatter.7.cloned.1.call-done = f32[1,16,7168]{2,1,0:T(8,128)} async-done(((f32[1,128,7168]{2,1,0:T(8,128)}), f32[1,16,7168]{2,1,0:T(8,128)}) %reduce-scatter.7.cloned.1.call-update) | async-done | bytes 458768 | tf_op jit(solution)/shard_map/reduce_scatter | solution.py:137
  846.1 3.3 fusion.6
  849.5 3.3 fusion.123
  (77 shorter events, 3.1 us)
Async XLA Ops:
  7.2 155.7 %copy-start = (bf16[1,1,7168,128]{3,2,1,0:T(8,128)(2,1)S(1)}, bf16[1,1,7168,128]{3,2,1,0:T(8,128)(2,1)}, u32[]{:S(2)}) copy-start(bf16[1,1,7168,128]{3,2,1,0:T(8,128)(2,1)} %param.20) | copy-start | bytes 5505028
  7.2 5.9 copy-start.4
  7.2 81.5 %all-gather.11.cloned.1.call-start = ((), (), s32[]{:S(2)}) async-start(), calls=%async_computation.11 | async-start | bytes 2064384 | tf_op jit(solution)/shard_map/all_gather | solution.py:131
  13.1 147.1 %all-gather.9.cloned.1.call-start = ((), (), s32[]{:S(2)}) async-start(), calls=%async_computation.10 | async-start | bytes 2064384 | tf_op jit(solution)/shard_map/all_gather | solution.py:132
  14.1 275.2 %reduce-scatter.9.cloned.1.call-start = ((), (), s32[]{:S(2)}) async-start(), calls=%async_computation.8 | async-start | bytes 4128768 | tf_op jit(solution)/shard_map/reduce_scatter | solution.py:138
  172.4 0.8 copy-start.7
  172.4 0.8 copy-start.8
  172.4 116.9 %copy-start.9 = (f32[1,7168]{1,0:T(1,128)S(1)}, f32[1,7168]{1,0:T(1,128)}, u32[]{:S(2)}) copy-start(f32[1,7168]{1,0:T(1,128)} %param.18) | copy-start | bytes 86020
  172.5 211.2 %all-gather.15.cloned.1.call-start = ((), (), s32[]{:S(2)}) async-start(), calls=%async_computation.13 | async-start | bytes 2064384 | tf_op jit(solution)/shard_map/all_gather | solution.py:131
  289.3 4.4 copy-start.1
  294.8 5.2 copy-start.5
  298.1 13.1 %collective-permute-start.1 = (bf16[64,7168]{1,0:T(8,128)(2,1)}, bf16[64,7168]{1,0:T(8,128)(2,1)}, u32[]{:S(2)}, u32[]{:S(2)}) collective-permute-start(bf16[64,7168]{1,0:T(8,128)(2,1)} %fusion.27), channel_id=1, source_target_pairs={{8,0},{16,8},{24,16},{32,24},{40,32},{48,40},{56,48},{64,56},{72,6... | collective-permute-start | bytes 2752520 | tf_op jit(solution)/shard_map/ppermute | solution.py:13
  301.9 9.3 %copy-start.3 = (bf16[1,64,7168]{2,1,0:T(8,128)(2,1)S(1)}, bf16[1,64,7168]{2,1,0:T(8,128)(2,1)}, u32[]{:S(2)}) copy-start(bf16[1,64,7168]{2,1,0:T(8,128)(2,1)} %param.16) | copy-start | bytes 2752516
  301.9 73.4 %all-to-all-start = ((bf16[8,1,16,7168]{3,2,1,0:T(8,128)(2,1)}), bf16[8,1,16,7168]{3,2,1,0:T(8,128)(2,1)}, u32[]{:S(2)}, u32[]{:S(2)}) async-start(bf16[8,1,16,7168]{3,2,1,0:T(8,128)(2,1)} %stack.4), calls=%async_computation | async-start | bytes 3670016 | tf_op jit(solution)/shard_map/all_to_all | solution.py:128
  306.4 149.1 %all-gather.13.cloned.1.call-start = ((), (), s32[]{:S(2)}) async-start(), calls=%async_computation.12 | async-start | bytes 2064384 | tf_op jit(solution)/shard_map/all_gather | solution.py:132
  313.4 263.3 %reduce-scatter.5.cloned.1.call-start = ((), (), s32[]{:S(2)}) async-start(), calls=%async_computation.6 | async-start | bytes 4128768 | tf_op jit(solution)/shard_map/reduce_scatter | solution.py:137
  383.2 342.7 %reduce-scatter.11.cloned.1.call-start = ((), (), s32[]{:S(2)}) async-start(), calls=%async_computation.9 | async-start | bytes 4128768 | tf_op jit(solution)/shard_map/reduce_scatter | solution.py:138
  580.0 15.0 %collective-permute-start = (bf16[64,7168]{1,0:T(8,128)(2,1)}, bf16[64,7168]{1,0:T(8,128)(2,1)}, u32[]{:S(2)}, u32[]{:S(2)}) collective-permute-start(bf16[64,7168]{1,0:T(8,128)(2,1)} %fusion.4), channel_id=1, source_target_pairs={{0,8},{8,16},{16,24},{24,32},{32,40},{40,48},{48,56},{56,64},{64,7... | collective-permute-start | bytes 2752520 | tf_op jit(solution)/shard_map/ppermute | solution.py:13
  596.9 0.9 copy-start.6
  599.7 46.9 %all-to-all-start.1 = ((bf16[8,1,16,7168]{3,2,1,0:T(8,128)(2,1)}), bf16[8,1,16,7168]{3,2,1,0:T(8,128)(2,1)}, u32[]{:S(2)}, u32[]{:S(2)}) async-start(bf16[8,1,16,7168]{3,2,1,0:T(8,128)(2,1)} %stack.5), calls=%async_computation.2 | async-start | bytes 3670016 | tf_op jit(solution)/shard_map/all_to_all | solution.py:128
  604.0 242.1 %reduce-scatter.7.cloned.1.call-start = ((), (), s32[]{:S(2)}) async-start(), calls=%async_computation.7 | async-start | bytes 4128768 | tf_op jit(solution)/shard_map/reduce_scatter | solution.py:137
  846.1 3.4 copy-start.2
Sparse Core Ops, SparseCore 0:
  13.2 75.4 all-gather.10
  91.9 68.2 all-gather.8
  172.6 116.6 reduce-scatter.8
  294.9 87.9 all-gather.14
  386.3 69.0 all-gather.12
  460.1 116.5 reduce-scatter.4
  581.0 144.7 reduce-scatter.10
  730.7 115.4 reduce-scatter.6
